TPU v7x, 512 devices: a whole 4x8x8 slice. The times are simulated.
512 devices in a mesh: frames: 16 (over y_hi, x, core), tiles: 32 (over y_lo, z).
Axes of the slice: x: 4, y: 8 (y_hi: 2, y_lo: 4; y = y_hi * 4 + y_lo), z: 8, core: 2. Of those that a mesh axis runs over, the one named last changes fastest.
Arguments:
- queries: bfloat16 [2, 32, 512, 3072], P(None, 'frames', 'tiles'), may hold values from -10 to 10
- keys: bfloat16 [2, 32, 512, 3072], P(None, 'frames', 'tiles'), may hold values from -4 to 4
- values: bfloat16 [2, 32, 512, 3072], P(None, 'frames', 'tiles'), may hold values from -6 to 6
- segment_ids: int32 [2, 32], replicated, may hold values from 0 to 15, never falling along the last dimension, each value on 1 to 3 neighbouring positions
Outputs:
- normed: bfloat16 [2, 32, 512, 3072], P(None, 'frames', 'tiles')
Inputs may be any that keep to these rules, and one draw needn't show every extreme that they name: `segment_ids`: non-decreasing along the frames of a clip, starting at 0 and rising by 0 or 1 from frame to frame; every value covers 1 to 3 consecutive frames.
All inputs are finite; a program needn't handle non-finite values.
Results may differ from a plain program's by a relative error of at most 0.012.
Values may be sent and summed in bfloat16 or wider, within the bound.
A program may use at most 128 MiB of HBM per device.

v0:
```python
import jax
import jax.numpy as jnp
from jax import lax
from jax.sharding import PartitionSpec as P

HEADS = 32
HD = 96


floor_score = -1e30


def block_mask(segment_ids, query_first, query_frames):
    query_ids = lax.dynamic_slice_in_dim(segment_ids, query_first, query_frames, 1)
    return segment_ids[:, None, :] <= query_ids[:, :, None]


def keep_state(previous):
    return previous


def attend_block(carried, query_rows, allowed, key_piece, value_piece, query_tokens):
    clip_count, key_frames, key_tokens, unused_width = key_piece.shape
    head_count = query_rows.shape[2]
    head_width = query_rows.shape[3]
    query_frames = allowed.shape[1]
    key_split = jnp.moveaxis(
        key_piece.reshape(clip_count, key_frames, key_tokens, head_count, head_width), 1, 0
    )
    value_split = jnp.moveaxis(
        value_piece.reshape(clip_count, key_frames, key_tokens, head_count, head_width), 1, 0
    )
    mask_split = jnp.moveaxis(allowed, 2, 0)

    def per_key_frame(state, items):
        key_rows, value_rows, frame_mask = items

        def update(previous):
            running_max, totals, summed_values = previous
            scores = jnp.einsum(
                "cqhd,ckhd->chqk", query_rows, key_rows, preferred_element_type=jnp.float32
            )
            scores = scores * head_width ** (-0.5)
            visible = jnp.broadcast_to(
                frame_mask[:, :, None], (clip_count, query_frames, query_tokens)
            )
            visible = visible.reshape(clip_count, 1, query_frames * query_tokens, 1)
            scores = jnp.where(visible, scores, floor_score)
            newest_max = jnp.maximum(running_max, jnp.max(scores, axis=-1))
            weights = jnp.where(visible, jnp.exp(scores - newest_max[..., None]), 0.0)
            rescale = jnp.exp(running_max - newest_max)
            totals = totals * rescale + jnp.sum(weights, axis=-1)
            increment = jnp.einsum(
                "chqk,ckhd->cqhd",
                weights.astype(jnp.bfloat16),
                value_rows,
                preferred_element_type=jnp.float32,
            )
            summed_values = summed_values * jnp.transpose(rescale, (0, 2, 1))[..., None] + increment
            return (newest_max, totals, summed_values)

        return (lax.cond(jnp.any(frame_mask), update, keep_state, state), None)

    final_state, unused = lax.scan(per_key_frame, carried, (key_split, value_split, mask_split))
    return final_state


def empty_state(clip_count, row_count, head_count, head_width):
    return (
        jnp.full((clip_count, head_count, row_count), floor_score, jnp.float32),
        jnp.zeros((clip_count, head_count, row_count), jnp.float32),
        jnp.zeros((clip_count, row_count, head_count, head_width), jnp.float32),
    )


def finish(carried, target_shape):
    running_max, totals, summed_values = carried
    context = summed_values / jnp.transpose(totals, (0, 2, 1))[..., None]
    return context.astype(jnp.bfloat16).reshape(target_shape)


def on_device(queries, keys, values, segment_ids):
    clip_count, frame_count, tile_tokens, feature_width = queries.shape
    head_count = HEADS // lax.axis_size("tiles")
    query_heads, key_heads, value_heads = (
        lax.all_to_all(queries, "tiles", split_axis=3, concat_axis=2, tiled=True),
        lax.all_to_all(keys, "tiles", split_axis=3, concat_axis=2, tiled=True),
        lax.all_to_all(values, "tiles", split_axis=3, concat_axis=2, tiled=True),
    )
    frame_tokens = query_heads.shape[2]
    group_index = lax.axis_index("frames")
    own_first = group_index * frame_count
    query_rows = query_heads.reshape(clip_count, frame_count * frame_tokens, head_count, HD)
    start_state = empty_state(clip_count, frame_count * frame_tokens, head_count, HD)
    key_piece = lax.all_gather(key_heads, "frames", axis=1, tiled=True)
    value_piece = lax.all_gather(value_heads, "frames", axis=1, tiled=True)
    own_mask = block_mask(segment_ids, own_first, frame_count)
    final_state = attend_block(
        start_state, query_rows, own_mask, key_piece, value_piece, frame_tokens
    )
    context = finish(final_state, query_heads.shape)
    token_layout = lax.all_to_all(context, "tiles", split_axis=2, concat_axis=3, tiled=True)
    context_wide = token_layout.astype(jnp.float32)
    inverse_rms = lax.rsqrt(jnp.mean(context_wide * context_wide, axis=-1, keepdims=True) + 1e-06)
    return (context_wide * inverse_rms).astype(jnp.bfloat16)


def solution(mesh):
    return jax.shard_map(
        on_device,
        mesh=mesh,
        in_specs=(
            P(None, "frames", "tiles", None),
            P(None, "frames", "tiles", None),
            P(None, "frames", "tiles", None),
            P(),
        ),
        out_specs=P(None, "frames", "tiles", None),
        check_vma=False,
    )
```

profile of v0, /device:TPU:63, one launch (start us, length us, event | category | flops | bytes accessed | tf_op | source)
XLA Modules:
  0.0 533.4 jit_solution(5888544936238465316)
XLA Ops:
  6.5 6.9 %copy.44 = bf16[2,2,16,3072]{2,1,0,3:T(2,128)(2,1)S(1)} copy(bf16[2,2,16,3072]{3,2,1,0:T(8,128)(2,1)} %param.9) | data formatting | bytes 786432 | tf_op args[1]
  16.8 26.9 %all_to_all.60 = bf16[32,2,3072]{2,1,0:T(2,128)(2,1)} all-to-all(bf16[32,2,3072]{2,1,0:T(2,128)(2,1)S(1)} %reshape.93), channel_id=1, replica_groups=mesh['frames'=16,'tiles'=32] {'tiles'}, dimensions={0} | all-to-all | bytes 786432 | tf_op jit(solution)/shard_map/all_to_all | solution.py:87
  43.8 10.1 %reshape.94 = bf16[3072,2,2,16]{3,2,1,0:T(2,128)(2,1)S(1)} reshape(bf16[32,2,3072]{2,1,0:T(2,128)(2,1)} %all_to_all.60) | data formatting | bytes 786432
  53.9 7.0 %copy.45 = bf16[2,2,16,32,96]{4,2,3,1,0:T(8,128)(2,1)} copy(bf16[2,2,16,32,96]{2,1,0,4,3:T(2,128)(2,1)S(1)} %bitcast.82) | data formatting | bytes 786432 | tf_op jit(solution)/shard_map/all_to_all | solution.py:87
  60.9 5.4 %copy.48 = bf16[2,2,16,3072]{2,1,0,3:T(2,128)(2,1)S(1)} copy(bf16[2,2,16,3072]{3,2,1,0:T(8,128)(2,1)S(1)} %copy-done) | data formatting | bytes 786432 | tf_op args[2]
  69.7 28.5 %all_to_all.61 = bf16[32,2,3072]{2,1,0:T(2,128)(2,1)} all-to-all(bf16[32,2,3072]{2,1,0:T(2,128)(2,1)S(1)} %reshape.97), channel_id=1, replica_groups=mesh['frames'=16,'tiles'=32] {'tiles'}, dimensions={0} | all-to-all | bytes 786432 | tf_op jit(solution)/shard_map/all_to_all | solution.py:88
  98.2 10.1 %reshape.98 = bf16[3072,2,2,16]{3,2,1,0:T(2,128)(2,1)S(1)} reshape(bf16[32,2,3072]{2,1,0:T(2,128)(2,1)} %all_to_all.61) | data formatting | bytes 786432
  108.4 7.0 %copy.49 = bf16[2,2,16,32,96]{4,2,3,1,0:T(8,128)(2,1)} copy(bf16[2,2,16,32,96]{2,1,0,4,3:T(2,128)(2,1)S(1)} %bitcast.83) | data formatting | bytes 786432 | tf_op jit(solution)/shard_map/all_to_all | solution.py:88
  115.4 5.4 %copy.46 = bf16[2,2,16,3072]{2,1,0,3:T(2,128)(2,1)S(1)} copy(bf16[2,2,16,3072]{3,2,1,0:T(8,128)(2,1)S(1)} %copy-done.1) | data formatting | bytes 786432 | tf_op args[0]
  124.8 7.3 %all-to-all-start.1 = ((bf16[32,2,3072]{2,1,0:T(2,128)(2,1)}), bf16[32,2,3072]{2,1,0:T(2,128)(2,1)S(1)}, u32[]{:S(2)}, u32[]{:S(2)}) async-start(bf16[32,2,3072]{2,1,0:T(2,128)(2,1)} %reshape.95), calls=%async_computation.1 | async-start | bytes 786432 | tf_op jit(solution)/shard_map/all_to_all | solution.py:86
  132.4 39.2 %all-to-all-done.1 = bf16[32,2,3072]{2,1,0:T(2,128)(2,1)S(1)} async-done(((bf16[32,2,3072]{2,1,0:T(2,128)(2,1)}), bf16[32,2,3072]{2,1,0:T(2,128)(2,1)S(1)}, u32[]{:S(2)}, u32[]{:S(2)}) %all-to-all-start.1) | async-done | bytes 393248 | tf_op jit(solution)/shard_map/all_to_all | solution.py:86
  173.9 7.0 %copy.47 = bf16[2,2,16,32,96]{4,2,3,1,0:T(8,128)(2,1)} copy(bf16[2,2,16,32,96]{2,1,0,4,3:T(2,128)(2,1)S(1)} %bitcast.84) | data formatting | bytes 786432 | tf_op jit(solution)/shard_map/all_to_all | solution.py:86
  182.2 10.6 %copy.50 = bf16[32,2,512,1,96]{2,4,1,3,0:T(8,128)(2,1)} copy(bf16[32,2,512,1,96]{4,2,0,1,3:T(8,128)(2,1)} %bitcast.88) | data formatting | bytes 12582912 | tf_op jit(solution)/shard_map/while | solution.py:64
  192.8 89.1 %all-gather.5.cloned.1.call-done = bf16[2,32,512,96]{3,2,1,0:T(8,128)(2,1)} async-done(((bf16[2,2,512,96]{3,2,1,0:T(8,128)(2,1)}), bf16[2,32,512,96]{3,2,1,0:T(8,128)(2,1)}) %all-gather.5.cloned.1.call-update) | async-done | bytes 6291472 | tf_op jit(solution)/shard_map/all_gather | solution.py:96
  281.9 10.7 %copy.52 = bf16[32,2,512,1,96]{2,4,1,3,0:T(8,128)(2,1)} copy(bf16[32,2,512,1,96]{4,2,0,1,3:T(8,128)(2,1)} %bitcast.89) | data formatting | bytes 12582912 | tf_op jit(solution)/shard_map/while | solution.py:64
  292.7 201.0 %while.14 = (s32[]{:T(128)}, f32[2,1,1024]{2,0,1:T(2,128)S(1)}, f32[2,1,1024]{2,0,1:T(2,128)S(1)}, f32[2,1024,1,96]{1,3,0,2:T(8,128)S(1)}, pred[32,2,2]{2,1,0:T(...) while((s32[]{:T(128)}, f32[2,1,1024]{2,0,1:T(2,128)S(1)}, ...), condition=%wide.region_6.7_spmd, body=%wide.region_0.6_spmd.sunk | while | flops 416684032 | bytes 15092971 | solution.py:64
  294.0 5.0 conditional.2
  300.3 5.0 conditional.2
  306.6 5.0 conditional.2
  312.9 5.0 conditional.2
  319.1 5.0 conditional.2
  325.4 5.0 conditional.2
  331.7 5.0 conditional.2
  338.0 5.0 conditional.2
  344.3 5.0 conditional.2
  350.6 5.0 conditional.2
  356.8 5.0 conditional.2
  363.1 5.0 conditional.2
  369.4 5.0 conditional.2
  375.7 5.0 conditional.2
  382.0 5.0 conditional.2
  388.3 5.0 conditional.2
  394.5 5.0 conditional.2
  400.8 5.0 conditional.2
  407.1 5.0 conditional.2
  413.4 5.0 conditional.2
  419.7 5.0 conditional.2
  425.9 5.0 conditional.2
  432.2 5.0 conditional.2
  438.5 5.0 conditional.2
  451.1 5.0 conditional.2
  457.4 5.0 conditional.2
  463.6 5.0 conditional.2
  469.9 5.0 conditional.2
  476.2 5.0 conditional.2
  482.5 5.0 conditional.2
  488.8 5.0 conditional.2
  495.0 29.2 %all_to_all.62 = bf16[2,2,512,96]{3,1,0,2:T(2,128)(2,1)S(1)} all-to-all(bf16[2,2,512,96]{3,1,0,2:T(2,128)(2,1)S(1)} %copy.53), channel_id=1, replica_groups=mesh['frames'=16,'tiles'=32] {'tiles'}, dimensions={2} | all-to-all | bytes 786432 | tf_op jit(solution)/shard_map/all_to_all | solution.py:102
  (322 shorter events, 201.1 us)
Async XLA Ops:
  6.5 175.6 %all-gather.3.cloned.1.call-start = ((), (), s32[]{:S(2)}) async-start(), calls=%async_computation.4 | async-start | bytes 8912896 | tf_op jit(solution)/shard_map/all_gather | solution.py:95
  43.8 17.2 %copy-start = (bf16[2,2,16,3072]{3,2,1,0:T(8,128)(2,1)S(1)}, bf16[2,2,16,3072]{3,2,1,0:T(8,128)(2,1)}, u32[]{:S(2)}) copy-start(bf16[2,2,16,3072]{3,2,1,0:T(8,128)(2,1)} %param.10) | copy-start | bytes 1179652
  60.9 221.1 %all-gather.5.cloned.1.call-start = ((), (), s32[]{:S(2)}) async-start(), calls=%async_computation.5 | async-start | bytes 8912896 | tf_op jit(solution)/shard_map/all_gather | solution.py:96
  98.2 17.1 %copy-start.1 = (bf16[2,2,16,3072]{3,2,1,0:T(8,128)(2,1)S(1)}, bf16[2,2,16,3072]{3,2,1,0:T(8,128)(2,1)}, u32[]{:S(2)}) copy-start(bf16[2,2,16,3072]{3,2,1,0:T(8,128)(2,1)} %param.8) | copy-start | bytes 1179652
  115.3 16.8 %copy-start.2 = (s32[2,32]{1,0:T(2,128)S(1)}, s32[2,32]{1,0:T(2,128)}, u32[]{:S(2)}) copy-start(s32[2,32]{1,0:T(2,128)} %param.11) | copy-start | bytes 772
  124.8 46.8 %all-to-all-start.1 = ((bf16[32,2,3072]{2,1,0:T(2,128)(2,1)}), bf16[32,2,3072]{2,1,0:T(2,128)(2,1)S(1)}, u32[]{:S(2)}, u32[]{:S(2)}) async-start(bf16[32,2,3072]{2,1,0:T(2,128)(2,1)} %reshape.95), calls=%async_computation.1 | async-start | bytes 786432 | tf_op jit(solution)/shard_map/all_to_all | solution.py:86
Sparse Core Ops, SparseCore 0:
  61.0 116.4 all-gather.2
  180.9 101.0 all-gather.4
where the time goes:
time: 537 us; the launch traced here: 533 us
  waiting for transfers between devices  128 us (24%)
  matrix products  122 us (23%)
  local copies, waits for them, and re-layouts  99.7 us (19%)
  blocking collectives  84.7 us (16%)
  other arithmetic  54.5 us (10%)
  loops' own time  23.2 us (4%)
  between operations  13.6 us (3%)
  starting transfers between devices  7.3 us (1%)
    all_gather x1, waiting for transfers between devices, on_device(): value_piece = lax.all_gather(value_heads, 'frames', axis=1, tiled=True)  89.1 us
    dot_general x32, matrix products, update(): jnp.einsum('chqk,ckhd->cqhd', weights.astype(jnp.bfloat16), value_rows, p...  66.7 us
    dot_general x32, matrix products, update(): jnp.einsum('cqhd,ckhd->chqk', query_rows, key_rows, preferred_element_typ...  55.2 us
    unnamed x15, local copies, waits for them, and re-layouts  51.1 us
    all_to_all x1, waiting for transfers between devices, on_device(): lax.all_to_all(queries, 'tiles', split_axis=3, concat_axis=2, tiled=True)  39.2 us
    reduce_sum x32, other arithmetic, update(): totals = totals * rescale + jnp.sum(weights, axis=-1)  31.4 us
    all_to_all x1, blocking collectives, on_device(): lax.all_to_all(context, 'tiles', split_axis=2, concat_axis=3, tiled=True)  29.2 us
    all_to_all x1, blocking collectives, on_device(): lax.all_to_all(values, 'tiles', split_axis=3, concat_axis=2, tiled=True)  28.5 us
  transfers between devices with their start and end apart: 3, of which 2 were waited for; matrix products, arithmetic and copies ran while one was open for 11% of the time, Pallas kernels for 0%

commit v1 on v0

v1 whole, which is shorter than its diff:
```python
import functools
import math

import jax
import jax.numpy as jnp
from jax import lax
from jax.experimental import pallas as pl
from jax.experimental.pallas import tpu as pltpu
from jax.sharding import PartitionSpec as P

MESH = pl.DeviceIdType.MESH
HD = 96
CLIPS = 2
NX, NCORE, NZ = 4, 2, 8
YH, YL = 2, 4
ND = NX * NCORE
GROUP = YL * HD
TOK = 16
RUN = NZ * TOK
FRAME_TOK = YL * RUN
NF = 2
FRAMES = YH * ND * NF
SCALE2 = HD ** (-0.5) * math.log2(math.e)
NF_Q = YH * NF
DEPTH = 256
LOW = -1e30
NT = (((1,), (1,)), ((), ()))


def place():
    fi = lax.axis_index("frames")
    ti = lax.axis_index("tiles")
    yh, d = fi // ND, fi % ND
    return yh, d, ti // NZ, ti % NZ


def dev(yh, d, yl, z):
    return (yh * ND + d, yl * NZ + z)


def greet(targets_of):
    barrier = pltpu.get_barrier_semaphore()
    total = 0
    for count, target in targets_of:
        total += count

        def one(k, carry, target=target):
            pl.semaphore_signal(barrier, inc=1, device_id=target(k), device_id_type=MESH)
            return carry

        lax.fori_loop(0, count, one, 0)
    pl.semaphore_wait(barrier, total)


def remote(src, dst, send, recv, target):
    return pltpu.make_async_remote_copy(
        src_ref=src, dst_ref=dst, send_sem=send, recv_sem=recv, device_id=target, device_id_type=MESH
    )


def kernel(
    seg, k_in, v_in, q_in, out, k_all, v_all, q_own, tokens, turned, rows_q, acc, top, scores, heads, feats, spun, rows,
    a_send, a_recv, b_send, b_recv, c_send, c_recv, d_send, d_recv, e_send, e_recv
):
    yh, d, yl, z = place()
    y = yh * YL + yl
    x, core = d // NCORE, d % NCORE
    up = lax.rem(x + 1, NX) * NCORE + core
    down = lax.rem(x + NX - 1, NX) * NCORE + core
    far = lax.rem(x + 2, NX) * NCORE + core
    twin = x * NCORE + 1 - core
    mirror = ND - 1 - d

    def z_peer(k):
        return lax.rem(z + 1 + k, NZ)

    def y_peer(k):
        yy = lax.rem(y + 1 + k, YH * YL)
        return yy // YL, lax.rem(yy, YL)

    greet(
        [
            (NZ - 1, lambda k: dev(yh, d, yl, z_peer(k))),
            (YH * YL - 1, lambda k: dev(y_peer(k)[0], d, y_peer(k)[1], z)),
            (YH * YL, lambda k: dev(k // YL, mirror, lax.rem(k, YL), z)),
            (1, lambda k: dev(yh, up, yl, z)),
            (1, lambda k: dev(yh, down, yl, z)),
            (1, lambda k: dev(yh, twin, yl, z)),
        ]
    )

    inputs = (k_in, v_in, q_in)
    chunks = [(0, 0), (1, 0), (2, 0), (2, 1), (0, 1), (1, 1)]
    key0, value0, query0, query1, key1, value1 = range(6)

    def a_src(t, zz):
        tensor, f = chunks[t]
        return inputs[tensor].at[:, f, :, pl.ds(pl.multiple_of(zz * GROUP, 128), GROUP)]

    def a_dst(t, zz):
        return tokens.at[t, :, pl.ds(pl.multiple_of(zz * TOK, TOK), TOK), :]

    def a_copy(t, k):
        zz = z_peer(k)
        return remote(a_src(t, zz), a_dst(t, z), a_send.at[t, zz], a_recv.at[t, z], dev(yh, d, yl, zz))

    def a_start(t):
        def one(k, carry):
            a_copy(t, k).start()
            return carry

        lax.fori_loop(0, NZ - 1, one, 0)
        pltpu.make_async_copy(a_src(t, z), a_dst(t, z), a_recv.at[t, z]).start()

    def a_wait(t):
        def one(zz, carry):
            pltpu.make_async_copy(a_src(t, zz), a_dst(t, zz), a_recv.at[t, zz]).wait()
            return carry

        lax.fori_loop(0, NZ, one, 0)

    def a_drain(t):
        def one(k, carry):
            a_copy(t, k).wait_send()
            return carry

        lax.fori_loop(0, NZ - 1, one, 0)

    def b_src(t, ch, hl):
        return turned.at[t, ch, pl.ds(pl.multiple_of(hl * HD, 32), HD), :]

    def b_dst(t, holder, h, l):
        tensor, f = chunks[t]
        lanes = pl.ds(pl.multiple_of(l * RUN, 128), RUN)
        if tensor == 2:
            return q_own.at[h, f, :, lanes]
        return (k_all, v_all)[tensor].at[h, holder, f, :, lanes]

    def b_copy(t, ch, hl, holder):
        return remote(
            b_src(t, ch, hl), b_dst(t, holder, yh, yl), b_send.at[t, ch * YL + hl], b_recv.at[t, y], dev(ch, holder, hl, z)
        )

    def b_start(t):
        for ch in range(CLIPS):
            turned[t, ch] = tokens[t, ch].T

        def one(k, carry):
            ch, hl = y_peer(k)
            if chunks[t][0] == 2:

                @pl.when(yh == 0)
                def _():
                    b_copy(t, ch, hl, d).start()

                @pl.when(yh == 1)
                def _():
                    b_copy(t, ch, hl, mirror).start()
            else:
                b_copy(t, ch, hl, d).start()
            return carry

        lax.fori_loop(0, YH * YL - 1, one, 0)
        own = pltpu.make_async_copy(b_src(t, yh, yl), b_dst(t, d, yh, yl), b_recv.at[t, y])
        if chunks[t][0] == 2:

            @pl.when(yh == 0)
            def _():
                own.start()

            @pl.when(yh == 1)
            def _():
                b_copy(t, yh, yl, mirror).start()
        else:
            own.start()

    def b_wait(t):
        def one(ys, carry):
            h, l = ys // YL, lax.rem(ys, YL)
            pltpu.make_async_copy(b_src(t, h, l), b_dst(t, d, h, l), b_recv.at[t, ys]).wait()
            return carry

        lax.fori_loop(0, YH * YL, one, 0)

    def b_drain(t):
        def one(k, carry):
            ch, hl = y_peer(k)
            b_copy(t, ch, hl, d).wait_send()
            return carry

        lax.fori_loop(0, YH * YL - 1, one, 0)
        if chunks[t][0] == 2:

            @pl.when(yh == 1)
            def _():
                b_copy(t, yh, yl, mirror).wait_send()

    def whole(t, holder):
        tensor, f = chunks[t]
        return (k_all, v_all)[tensor].at[:, holder, f]

    def half(t, holder, h):
        tensor, f = chunks[t]
        return (k_all, v_all)[tensor].at[h, holder, f]

    def c_copy(t, kind):
        ref, there = {
            0: (lambda: whole(t, d), up),
            1: (lambda: whole(t, d), down),
            2: (lambda: half(t, down, 0), up),
            3: (lambda: half(t, up, 1), down),
            4: (lambda: whole(t, d), twin),
            5: (lambda: whole(t, down), twin),
            6: (lambda: whole(t, up), twin),
            7: (lambda: half(t, far, 0), twin),
            8: (lambda: half(t, far, 1), twin),
        }[kind]
        ref = ref()
        return remote(ref, ref, c_send.at[t, kind], c_recv.at[t, kind], dev(yh, there, yl, z))

    def c_arrived(t, kind):
        far_twin = lax.rem(x + 2, NX) * NCORE + 1 - core
        up_twin = lax.rem(x + 1, NX) * NCORE + 1 - core
        down_twin = lax.rem(x + NX - 1, NX) * NCORE + 1 - core
        ref = {
            0: lambda: whole(t, down),
            1: lambda: whole(t, up),
            2: lambda: half(t, far, 0),
            3: lambda: half(t, far, 1),
            4: lambda: whole(t, twin),
            5: lambda: whole(t, down_twin),
            6: lambda: whole(t, up_twin),
            7: lambda: half(t, far_twin, 0),
            8: lambda: half(t, far_twin, 1),
        }[kind]()
        pltpu.make_async_copy(ref, ref, c_recv.at[t, kind]).wait()

    def c_start(t):
        b_wait(t)
        for kind in (0, 1, 4):
            c_copy(t, kind).start()

    def c_relay(t):
        c_arrived(t, 0)
        c_copy(t, 2).start()
        c_copy(t, 5).start()
        c_arrived(t, 1)
        c_copy(t, 3).start()
        c_copy(t, 6).start()

    def c_last(t):
        for kind in (2, 3):
            c_arrived(t, kind)
            c_copy(t, kind + 5).start()

    def c_end(t):
        for kind in range(9):
            c_copy(t, kind).wait_send()

    def query_frame(i):
        h, f = i // NF, i % NF
        return jnp.where(h == 0, d, YH * ND - 1 - d) * NF + f

    def prepare():
        spare = lax.broadcasted_iota(jnp.int32, (DEPTH - 2 * HD, FRAME_TOK), 0)
        flag = jnp.where(spare == 0, 1.0, 0.0).astype(jnp.bfloat16)
        for i in range(NF_Q):
            scaled = q_own[i // NF, i % NF].astype(jnp.float32) * SCALE2
            high = scaled.astype(jnp.bfloat16)
            low = (scaled - high.astype(jnp.float32)).astype(jnp.bfloat16)
            rows_q[i] = jnp.concatenate([high, low, flag], axis=0).T
            acc[i] = jnp.zeros(acc.shape[1:], jnp.float32)
            top[i] = jnp.full(top.shape[1:], LOW, jnp.float32)

    ones = jnp.ones((128 - HD, FRAME_TOK), jnp.bfloat16)
    spare_row = lax.broadcasted_iota(jnp.int32, (DEPTH - 2 * HD, FRAME_TOK), 0)

    def unit(i, h, xs, f):
        own_id = seg[yh, query_frame(i)]
        highest = None
        for c in range(NCORE):
            holder = xs * NCORE + c
            bias = jnp.where(seg[yh, (h * ND + holder) * NF + f] <= own_id, 0.0, LOW)
            block = k_all[h, holder, f]
            extra = jnp.where(spare_row == 0, bias, 0.0).astype(jnp.bfloat16)
            s = jnp.dot(
                rows_q[i], jnp.concatenate([block, block, extra], axis=0), preferred_element_type=jnp.float32
            )
            scores[c] = s
            for lane in range(0, FRAME_TOK, 128):
                part = s[:, lane : lane + 128]
                highest = part if highest is None else jnp.maximum(highest, part)
        before = top[i]
        newest = jnp.maximum(before, jnp.max(highest, axis=1, keepdims=True))
        top[i] = newest
        wide = jnp.concatenate([newest] * (FRAME_TOK // 128), axis=1)
        total = acc[i] * jnp.exp2(before - newest)
        for c in range(NCORE):
            p = jnp.exp2(scores[c] - wide).astype(jnp.bfloat16)
            block = jnp.concatenate([v_all[h, xs * NCORE + c, f], ones], axis=0)
            total += lax.dot_general(p, block, NT, preferred_element_type=jnp.float32)
        acc[i] = total

    def visit(xs, f):
        def one(n, carry):
            h, i = n // NF_Q, lax.rem(n, NF_Q)

            @pl.when((h * ND + xs * NCORE) * NF + f <= query_frame(i) + 2)
            def _():
                unit(i, h, xs, f)

            return carry

        lax.fori_loop(0, YH * NF_Q, one, 0)

    def sweep(i, f, first, last):
        def one(n, carry):
            unit(i, n // NX, lax.rem(n, NX), f)
            return carry

        seen = (query_frame(i) + 2 - f) // (NCORE * NF) + 1
        lax.fori_loop(first, jnp.minimum(seen, last), one, 0)

    def d_src(i, l):
        return heads.at[i, :, pl.ds(pl.multiple_of(l * RUN, 128), RUN)]

    def d_dst(f, clip, hl):
        return feats.at[f, clip, pl.ds(pl.multiple_of(hl * HD, 32), HD), :]

    def d_copy(i, l):
        h, f = i // NF, i % NF
        there = d if h == 0 else mirror
        return remote(d_src(i, l), d_dst(f, yh, yl), d_send.at[i, l], d_recv.at[f, y], dev(h, there, l, z))

    def d_run(i, act):
        def one(k, carry):
            act(d_copy(i, lax.rem(yl + 1 + k, YL)))
            return carry

        lax.fori_loop(0, YL - 1, one, 0)

    def d_start(i):
        total = acc[i]
        heads[i] = (total[:, :HD] / total[:, HD : HD + 1]).astype(jnp.bfloat16).T
        d_run(i, lambda copy: copy.start())
        if i < NF:

            @pl.when(yh == 0)
            def _():
                pltpu.make_async_copy(d_src(i, yl), d_dst(i, yh, yl), d_recv.at[i, y]).start()

            @pl.when(yh == 1)
            def _():
                d_copy(i, yl).start()
        else:
            d_copy(i, yl).start()

    def d_wait(f):
        def one(ys, carry):
            c, l = ys // YL, lax.rem(ys, YL)
            pltpu.make_async_copy(d_src(f, l), d_dst(f, c, l), d_recv.at[f, ys]).wait()
            return carry

        lax.fori_loop(0, YH * YL, one, 0)

    def d_drain(i):
        d_run(i, lambda copy: copy.wait_send())
        if i < NF:

            @pl.when(yh == 1)
            def _():
                d_copy(i, yl).wait_send()
        else:
            d_copy(i, yl).wait_send()

    def e_src(f, zz):
        return spun.at[f, :, pl.ds(pl.multiple_of(zz * TOK, TOK), TOK), :]

    def e_dst(f, zz):
        return rows.at[:, f, :, pl.ds(pl.multiple_of(zz * GROUP, 128), GROUP)]

    def e_copy(f, k):
        zz = z_peer(k)
        return remote(e_src(f, zz), e_dst(f, z), e_send.at[f, zz], e_recv.at[f, z], dev(yh, d, yl, zz))

    def e_run(f, act):
        def one(k, carry):
            act(e_copy(f, k))
            return carry

        lax.fori_loop(0, NZ - 1, one, 0)

    def e_start(f):
        d_wait(f)
        for clip in range(CLIPS):
            spun[f, clip] = feats[f, clip].T
        pltpu.make_async_copy(e_src(f, z), e_dst(f, z), e_recv.at[f, z]).start()
        e_run(f, lambda copy: copy.start())

    def e_finish(f):
        def one(zz, carry):
            pltpu.make_async_copy(e_src(f, zz), e_dst(f, zz), e_recv.at[f, zz]).wait()
            return carry

        lax.fori_loop(0, NZ, one, 0)
        for clip in range(CLIPS):
            context = rows[clip, f].astype(jnp.float32)
            inverse_rms = lax.rsqrt(jnp.mean(context * context, axis=-1, keepdims=True) + 1e-06)
            out[clip, f] = (context * inverse_rms).astype(jnp.bfloat16)

    for t in range(6):
        a_start(t)
    a_wait(key0)
    b_start(key0)
    a_wait(value0)
    b_start(value0)
    c_start(key0)
    a_wait(query0)
    b_start(query0)
    c_start(value0)
    a_wait(query1)
    b_start(query1)
    c_relay(key0)
    a_wait(key1)
    b_start(key1)
    c_relay(value0)
    a_wait(value1)
    b_start(value1)
    b_wait(query0)
    b_wait(query1)
    prepare()
    x_up, x_down, x_far = lax.rem(x + 1, NX), lax.rem(x + NX - 1, NX), lax.rem(x + 2, NX)

    def ready(f, kinds):
        for t in ((key0, value0), (key1, value1))[f]:
            for kind in kinds:
                c_arrived(t, kind)

    c_start(key1)
    c_last(key0)
    ready(0, (4,))
    visit(x, 0)
    c_start(value1)
    c_last(value0)
    ready(0, (5,))
    visit(x_down, 0)
    c_relay(key1)
    ready(0, (6,))
    visit(x_up, 0)
    c_relay(value1)
    c_last(key1)
    ready(0, (7, 8))
    visit(x_far, 0)
    c_last(value1)
    ready(1, (4, 5, 6, 7, 8))
    for i in range(NF_Q - 1):
        sweep(i, 1, 0, YH * NX)
        d_start(i)
    sweep(NF_Q - 1, 1, 0, 4)
    e_start(0)
    sweep(NF_Q - 1, 1, 4, YH * NX)
    d_start(NF_Q - 1)
    e_start(1)
    e_finish(0)
    e_finish(1)
    for t in range(6):
        a_drain(t)
        b_drain(t)
        if chunks[t][0] < 2:
            c_end(t)
    for i in range(NF_Q):
        d_drain(i)
    for f in range(NF):
        e_run(f, lambda copy: copy.wait_send())


def on_device(queries, keys, values, segment_ids):
    hbm = pl.BlockSpec(memory_space=pltpu.HBM)
    vmem = pl.BlockSpec(memory_space=pltpu.VMEM)
    gathered = pltpu.VMEM((YH, ND, NF, HD, FRAME_TOK), jnp.bfloat16)
    state = pltpu.VMEM((NF_Q, FRAME_TOK, 128), jnp.float32)
    dma = pltpu.SemaphoreType.DMA
    return pl.pallas_call(
        kernel,
        out_shape=jax.ShapeDtypeStruct((CLIPS, NF, TOK, NZ * GROUP), jnp.bfloat16),
        in_specs=[pl.BlockSpec(memory_space=pltpu.SMEM), hbm, hbm, hbm],
        out_specs=vmem,
        scratch_shapes=[
            gathered,
            gathered,
            pltpu.VMEM((YH, NF, HD, FRAME_TOK), jnp.bfloat16),
            pltpu.VMEM((6, CLIPS, RUN, GROUP), jnp.bfloat16),
            pltpu.VMEM((6, CLIPS, GROUP, RUN), jnp.bfloat16),
            pltpu.VMEM((NF_Q, FRAME_TOK, DEPTH), jnp.bfloat16),
            state,
            state,
            pltpu.VMEM((NCORE, FRAME_TOK, FRAME_TOK), jnp.float32),
            pltpu.VMEM((NF_Q, HD, FRAME_TOK), jnp.bfloat16),
            pltpu.VMEM((NF, CLIPS, GROUP, RUN), jnp.bfloat16),
            pltpu.VMEM((NF, CLIPS, RUN, GROUP), jnp.bfloat16),
            pltpu.VMEM((CLIPS, NF, TOK, NZ * GROUP), jnp.bfloat16),
            dma((6, NZ)),
            dma((6, NZ)),
            dma((6, YH * YL)),
            dma((6, YH * YL)),
            dma((6, 9)),
            dma((6, 9)),
            dma((NF_Q, YL)),
            dma((NF, YH * YL)),
            dma((NF, NZ)),
            dma((NF, NZ)),
        ],
        compiler_params=pltpu.CompilerParams(collective_id=0, has_side_effects=True, vmem_limit_bytes=56 << 20),
        name="attend",
    )(segment_ids, keys, values, queries)


def solution(mesh):
    rows = P(None, "frames", "tiles", None)
    return jax.shard_map(
        on_device,
        mesh=mesh,
        in_specs=(rows, rows, rows, P()),
        out_specs=rows,
        check_vma=False,
    )
```

time: 537 us -> 117 us (0.22)
  the two profiles are of different devices: /device:TPU:63 before, /device:TPU:56 now
where the time goes in v1:
time: 117 us; the launch traced here: 116 us
  Pallas kernels  114 us (97%)
  local copies, waits for them, and re-layouts  1.77 us (2%)
    pallas_call x1, Pallas kernels, on_device(): pl.pallas_call(kernel, out_shape=jax.ShapeDtypeStruct((CLIPS, NF, TOK, NZ...  114 us

profile of v1, /device:TPU:56, one launch (start us, length us, event | category | flops | bytes accessed | tf_op | source)
XLA Modules:
  0.0 116.0 jit_solution(8747734501964398193)
XLA Ops:
  0.0 114.2 %attend.1 = bf16[2,2,16,3072]{3,2,1,0:T(8,128)(2,1)} custom-call(s32[2,32]{1,0:T(2,128)} %seg.1, bf16[2,2,16,3072]{3,2,1,0:T(8,128)(2,1)} %k_in.1, bf16[2,2,16,3072]{3,2,1,0:T(8,128)(2,1)} %v_in.1, bf16[2,2,16,3072]{3,2,1,0:T(8,128)(2,1)} %q_in.1), custom_call_target="tpu_custom_call" | custom-call | tf_op jit(solution)/shard_map/attend/pallas_call | solution.py:483
  114.2 1.8 %copy.6 = bf16[2,2,16,3072]{3,2,1,0:T(8,128)(2,1)} copy(bf16[2,2,16,3072]{3,2,1,0:T(8,128)(2,1)} %attend.1) | data formatting | bytes 786432

commit v2 on v1

--- a/solution.py
+++ b/solution.py
@@ -275,20 +275,21 @@
     ones = jnp.ones((128 - HD, FRAME_TOK), jnp.bfloat16)
     spare_row = lax.broadcasted_iota(jnp.int32, (DEPTH - 2 * HD, FRAME_TOK), 0)
 
-    def unit(i, h, xs, f):
+    def score(i, h, xs, f, slot):
         own_id = seg[yh, query_frame(i)]
-        highest = None
         for c in range(NCORE):
             holder = xs * NCORE + c
             bias = jnp.where(seg[yh, (h * ND + holder) * NF + f] <= own_id, 0.0, LOW)
             block = k_all[h, holder, f]
             extra = jnp.where(spare_row == 0, bias, 0.0).astype(jnp.bfloat16)
-            s = jnp.dot(
-                rows_q[i], jnp.concatenate([block, block, extra], axis=0), preferred_element_type=jnp.float32
-            )
-            scores[c] = s
+            block = jnp.concatenate([block, block, extra], axis=0)
+            scores[slot, c] = jnp.dot(rows_q[i], block, preferred_element_type=jnp.float32)
+
+    def weigh(i, h, xs, f, slot):
+        highest = None
+        for c in range(NCORE):
             for lane in range(0, FRAME_TOK, 128):
-                part = s[:, lane : lane + 128]
+                part = scores[slot, c, :, lane : lane + 128]
                 highest = part if highest is None else jnp.maximum(highest, part)
         before = top[i]
         newest = jnp.maximum(before, jnp.max(highest, axis=1, keepdims=True))
@@ -296,29 +297,37 @@
         wide = jnp.concatenate([newest] * (FRAME_TOK // 128), axis=1)
         total = acc[i] * jnp.exp2(before - newest)
         for c in range(NCORE):
-            p = jnp.exp2(scores[c] - wide).astype(jnp.bfloat16)
+            p = jnp.exp2(scores[slot, c] - wide).astype(jnp.bfloat16)
             block = jnp.concatenate([v_all[h, xs * NCORE + c, f], ones], axis=0)
             total += lax.dot_general(p, block, NT, preferred_element_type=jnp.float32)
         acc[i] = total
 
     def visit(xs, f):
         def one(n, carry):
-            h, i = n // NF_Q, lax.rem(n, NF_Q)
-
-            @pl.when((h * ND + xs * NCORE) * NF + f <= query_frame(i) + 2)
-            def _():
-                unit(i, h, xs, f)
-
-            return carry
-
-        lax.fori_loop(0, YH * NF_Q, one, 0)
+            h, pair = n // YH, lax.rem(n, YH)
+            i = pair * NF
+
+            @pl.when((h * ND + xs * NCORE) * NF + f <= query_frame(i + 1) + 2)
+            def _():
+                score(i, h, xs, f, 0)
+                score(i + 1, h, xs, f, 1)
+                weigh(i, h, xs, f, 0)
+                weigh(i + 1, h, xs, f, 1)
+
+            return carry
+
+        lax.fori_loop(0, YH * YH, one, 0)
 
     def sweep(i, f, first, last):
         def one(n, carry):
-            unit(i, n // NX, lax.rem(n, NX), f)
-            return carry
-
-        seen = (query_frame(i) + 2 - f) // (NCORE * NF) + 1
+            h, xs = n // (NX // 2), lax.rem(n, NX // 2) * 2
+            score(i, h, xs, f, 0)
+            score(i, h, xs + 1, f, 1)
+            weigh(i, h, xs, f, 0)
+            weigh(i, h, xs + 1, f, 1)
+            return carry
+
+        seen = (query_frame(i) + 2 - f) // (2 * NCORE * NF) + 1
         lax.fori_loop(first, jnp.minimum(seen, last), one, 0)
 
     def d_src(i, l):
@@ -454,11 +463,11 @@
     c_last(value1)
     ready(1, (4, 5, 6, 7, 8))
     for i in range(NF_Q - 1):
-        sweep(i, 1, 0, YH * NX)
+        sweep(i, 1, 0, YH * NX // 2)
         d_start(i)
-    sweep(NF_Q - 1, 1, 0, 4)
+    sweep(NF_Q - 1, 1, 0, 2)
     e_start(0)
-    sweep(NF_Q - 1, 1, 4, YH * NX)
+    sweep(NF_Q - 1, 1, 2, YH * NX // 2)
     d_start(NF_Q - 1)
     e_start(1)
     e_finish(0)
@@ -494,7 +503,7 @@
             pltpu.VMEM((NF_Q, FRAME_TOK, DEPTH), jnp.bfloat16),
             state,
             state,
-            pltpu.VMEM((NCORE, FRAME_TOK, FRAME_TOK), jnp.float32),
+            pltpu.VMEM((2, NCORE, FRAME_TOK, FRAME_TOK), jnp.float32),
             pltpu.VMEM((NF_Q, HD, FRAME_TOK), jnp.bfloat16),
             pltpu.VMEM((NF, CLIPS, GROUP, RUN), jnp.bfloat16),
             pltpu.VMEM((NF, CLIPS, RUN, GROUP), jnp.bfloat16),

time: 117 us -> 104 us (0.89)
  Pallas kernels: 114 us -> 102 us
    pallas_call x1, Pallas kernels: 114 us -> 102 us  [on_device(): pl.pallas_call(kernel, out_shape=jax.ShapeDtypeStruct((CLIPS, NF, TOK, NZ...]
where the time goes in v2:
time: 104 us
  Pallas kernels  102 us (98%)
  local copies, waits for them, and re-layouts  1.77 us (2%)
    pallas_call x1, Pallas kernels, on_device(): pl.pallas_call(kernel, out_shape=jax.ShapeDtypeStruct((CLIPS, NF, TOK, NZ...  102 us

profile of v2, /device:TPU:56, one launch (start us, length us, event | category | flops | bytes accessed | tf_op | source)
XLA Modules:
  0.0 103.6 jit_solution(11349962559696486735)
XLA Ops:
  0.0 101.8 %attend.1 = bf16[2,2,16,3072]{3,2,1,0:T(8,128)(2,1)} custom-call(s32[2,32]{1,0:T(2,128)} %seg.1, bf16[2,2,16,3072]{3,2,1,0:T(8,128)(2,1)} %k_in.1, bf16[2,2,16,3072]{3,2,1,0:T(8,128)(2,1)} %v_in.1, bf16[2,2,16,3072]{3,2,1,0:T(8,128)(2,1)} %q_in.1), custom_call_target="tpu_custom_call" | custom-call | tf_op jit(solution)/shard_map/attend/pallas_call | solution.py:492
  101.8 1.8 %copy.6 = bf16[2,2,16,3072]{3,2,1,0:T(8,128)(2,1)} copy(bf16[2,2,16,3072]{3,2,1,0:T(8,128)(2,1)} %attend.1) | data formatting | bytes 786432

commit v3 on v2

v3 whole, which is shorter than its diff:
```python
import functools
import math

import jax
import jax.numpy as jnp
from jax import lax
from jax.experimental import pallas as pl
from jax.experimental.pallas import tpu as pltpu
from jax.sharding import PartitionSpec as P

MESH = pl.DeviceIdType.MESH
HD = 96
CLIPS = 2
NX, NCORE, NZ = 4, 2, 8
YH, YL = 2, 4
ND = NX * NCORE
GROUP = YL * HD
TOK = 16
RUN = NZ * TOK
FRAME_TOK = YL * RUN
NF = 2
FRAMES = YH * ND * NF
SCALE2 = HD ** (-0.5) * math.log2(math.e)
NF_Q = YH * NF
DEPTH = 256
LOW = -1e30
NT = (((1,), (1,)), ((), ()))


def place():
    fi = lax.axis_index("frames")
    ti = lax.axis_index("tiles")
    yh, d = fi // ND, fi % ND
    return yh, d, ti // NZ, ti % NZ


def dev(yh, d, yl, z):
    return (yh * ND + d, yl * NZ + z)


def greet(partners):
    barrier = pltpu.get_barrier_semaphore()
    for partner in partners:
        pl.semaphore_signal(barrier, inc=1, device_id=partner, device_id_type=MESH)
    pl.semaphore_wait(barrier, len(partners))


def take(ref, semaphore):
    pltpu.make_async_copy(ref, ref, semaphore).wait()


def remote(src, dst, send, recv, target):
    return pltpu.make_async_remote_copy(
        src_ref=src, dst_ref=dst, send_sem=send, recv_sem=recv, device_id=target, device_id_type=MESH
    )


def kernel(
    seg, k_in, v_in, q_in, out, k_all, v_all, q_own, tokens, tokens_q, turned, turned_q, rows_q, acc, top, scores,
    heads, feats, spun, rows, a_send, a_recv, b_send, b_recv, c_send, c_recv, d_send, d_recv, e_send, e_recv
):
    yh, d, yl, z = place()
    y = yh * YL + yl
    x, core = d // NCORE, d % NCORE
    up = lax.rem(x + 1, NX) * NCORE + core
    down = lax.rem(x + NX - 1, NX) * NCORE + core
    far = lax.rem(x + 2, NX) * NCORE + core
    twin = x * NCORE + 1 - core
    mirror = ND - 1 - d
    z_peers = [lax.rem(z + k, NZ) for k in range(1, NZ)]
    y_peers = [(yy // YL, lax.rem(yy, YL)) for yy in [lax.rem(y + k, YH * YL) for k in range(1, YH * YL)]]

    greet(
        [dev(yh, d, yl, zz) for zz in z_peers]
        + [dev(h, d, l, z) for h, l in y_peers]
        + [dev(h, mirror, l, z) for h in range(YH) for l in range(YL)]
        + [dev(yh, there, yl, z) for there in (up, down, twin)]
    )

    key0, value0, query, key1, value1 = range(5)
    arrays = (k_all, v_all, None, k_all, v_all)
    inputs = (k_in, v_in, q_in, k_in, v_in)
    frame_of = (0, 0, None, 1, 1)

    def a_src(t, zz):
        lanes = pl.ds(pl.multiple_of(zz * GROUP, 128), GROUP)
        if t == query:
            return q_in.at[:, :, :, lanes]
        return inputs[t].at[:, frame_of[t], :, lanes]

    def a_dst(t, first, count):
        run = pl.ds(pl.multiple_of(first, TOK), count)
        if t == query:
            return tokens_q.at[:, :, run, :]
        return tokens.at[t, :, run, :]

    def a_start(t):
        mine = a_dst(t, z * TOK, TOK)
        for zz in z_peers:
            remote(a_src(t, zz), mine, a_send.at[t], a_recv.at[t], dev(yh, d, yl, zz)).start()
        pltpu.make_async_copy(a_src(t, z), mine, a_recv.at[t]).start()

    def a_wait(t):
        take(a_dst(t, 0, RUN), a_recv.at[t])

    def a_drain(t):
        take(a_dst(t, 0, RUN - TOK), a_send.at[t])

    def b_src(t, first, count):
        run = pl.ds(pl.multiple_of(first, 32), count)
        if t == query:
            return turned_q.at[:, run, :]
        return turned.at[t, run, :]

    def b_dst(t, h, l):
        lanes = pl.ds(pl.multiple_of(l * RUN, 128), RUN)
        if t == query:
            return q_own.at[h, :, :, lanes]
        return arrays[t].at[h, d, frame_of[t], :, lanes]

    def b_copy(t, h, l, holder):
        block = b_src(t, (h * YL + l) * HD, HD)
        return remote(block, b_dst(t, yh, yl), b_send.at[t], b_recv.at[t], dev(h, holder, l, z))

    def b_start(t):
        own = pltpu.make_async_copy(b_src(t, y * HD, HD), b_dst(t, yh, yl), b_recv.at[t])
        for clip in range(CLIPS):
            part = slice(clip * GROUP, (clip + 1) * GROUP)
            if t == query:
                for f in range(NF):
                    turned_q[f, part] = tokens_q[clip, f].T
            else:
                turned[t, part] = tokens[t, clip].T
        if t == query:

            @pl.when(yh == 0)
            def _():
                for h, l in y_peers:
                    b_copy(t, h, l, d).start()
                own.start()

            @pl.when(yh == 1)
            def _():
                for h, l in y_peers:
                    b_copy(t, h, l, mirror).start()
                b_copy(t, yh, yl, mirror).start()
        else:
            for h, l in y_peers:
                b_copy(t, h, l, d).start()
            own.start()

    def b_wait(t):
        take(q_own if t == query else whole(t, d), b_recv.at[t])

    def b_drain(t):
        most, every = CLIPS * GROUP - HD, CLIPS * GROUP
        if t == query:

            @pl.when(yh == 0)
            def _():
                take(b_src(t, 0, most), b_send.at[t])

            @pl.when(yh == 1)
            def _():
                take(b_src(t, 0, every), b_send.at[t])
        else:
            take(b_src(t, 0, most), b_send.at[t])

    def whole(t, holder):
        return arrays[t].at[:, holder, frame_of[t]]

    def half(t, holder, h):
        return arrays[t].at[h, holder, frame_of[t]]

    def c_copy(t, kind, ref, there):
        remote(ref, ref, c_send.at[t], c_recv.at[t, kind], dev(yh, there, yl, z)).start()

    def c_start(t):
        b_wait(t)
        c_copy(t, 0, whole(t, d), up)
        c_copy(t, 1, whole(t, d), down)
        c_copy(t, 4, whole(t, d), twin)

    def c_relay(t):
        take(whole(t, down), c_recv.at[t, 0])
        c_copy(t, 2, half(t, down, 0), up)
        c_copy(t, 5, whole(t, down), twin)
        take(whole(t, up), c_recv.at[t, 1])
        c_copy(t, 3, half(t, up, 1), down)
        c_copy(t, 6, whole(t, up), twin)

    def c_last(t):
        take(half(t, far, 0), c_recv.at[t, 2])
        c_copy(t, 7, half(t, far, 0), twin)
        take(half(t, far, 1), c_recv.at[t, 3])
        c_copy(t, 7, half(t, far, 1), twin)

    def c_ready(f, kind):
        for t in ((key0, value0), (key1, value1))[f]:
            take(whole(t, twin), c_recv.at[t, kind])

    def c_drain(t):
        take(arrays[t].at[:, pl.ds(0, 7), frame_of[t]], c_send.at[t])

    def query_frame(i):
        h, f = i // NF, i % NF
        return jnp.where(h == 0, d, YH * ND - 1 - d) * NF + f

    def prepare():
        spare = lax.broadcasted_iota(jnp.int32, (DEPTH - 2 * HD, FRAME_TOK), 0)
        flag = jnp.where(spare == 0, 1.0, 0.0).astype(jnp.bfloat16)
        for i in range(NF_Q):
            scaled = q_own[i // NF, i % NF].astype(jnp.float32) * SCALE2
            high = scaled.astype(jnp.bfloat16)
            low = (scaled - high.astype(jnp.float32)).astype(jnp.bfloat16)
            rows_q[i] = jnp.concatenate([high, low, flag], axis=0).T
            acc[i] = jnp.zeros(acc.shape[1:], jnp.float32)
            top[i] = jnp.full(top.shape[1:], LOW, jnp.float32)

    ones = jnp.ones((128 - HD, FRAME_TOK), jnp.bfloat16)
    spare_row = lax.broadcasted_iota(jnp.int32, (DEPTH - 2 * HD, FRAME_TOK), 0)

    def score(i, h, xs, f, slot):
        own_id = seg[yh, query_frame(i)]
        for c in range(NCORE):
            holder = xs * NCORE + c
            bias = jnp.where(seg[yh, (h * ND + holder) * NF + f] <= own_id, 0.0, LOW)
            block = k_all[h, holder, f]
            extra = jnp.where(spare_row == 0, bias, 0.0).astype(jnp.bfloat16)
            block = jnp.concatenate([block, block, extra], axis=0)
            scores[slot, c] = jnp.dot(rows_q[i], block, preferred_element_type=jnp.float32)

    def weigh(i, h, xs, f, slot):
        highest = None
        for c in range(NCORE):
            for lane in range(0, FRAME_TOK, 128):
                part = scores[slot, c, :, lane : lane + 128]
                highest = part if highest is None else jnp.maximum(highest, part)
        before = top[i]
        newest = jnp.maximum(before, jnp.max(highest, axis=1, keepdims=True))
        top[i] = newest
        wide = jnp.concatenate([newest] * (FRAME_TOK // 128), axis=1)
        total = acc[i] * jnp.exp2(before - newest)
        for c in range(NCORE):
            p = jnp.exp2(scores[slot, c] - wide).astype(jnp.bfloat16)
            block = jnp.concatenate([v_all[h, xs * NCORE + c, f], ones], axis=0)
            total += lax.dot_general(p, block, NT, preferred_element_type=jnp.float32)
        acc[i] = total

    def visit(xs, f):
        def one(n, carry):
            h, i = lax.rem(n, YH), n // YH * NF

            @pl.when((h * ND + xs * NCORE) * NF + f <= query_frame(i + 1) + 2)
            def _():
                score(i, h, xs, f, 0)
                score(i + 1, h, xs, f, 1)
                weigh(i, h, xs, f, 0)
                weigh(i + 1, h, xs, f, 1)

            return carry

        lax.fori_loop(0, YH * YH, one, 0)

    def sweep(i, f, first, last):
        def one(n, carry):
            h, xs = n // (NX // 2), lax.rem(n, NX // 2) * 2
            score(i, h, xs, f, 0)
            score(i, h, xs + 1, f, 1)
            weigh(i, h, xs, f, 0)
            weigh(i, h, xs + 1, f, 1)
            return carry

        seen = (query_frame(i) + 2 - f) // (2 * NCORE * NF) + 1
        lax.fori_loop(first, jnp.minimum(seen, last), one, 0)

    def d_src(i, first, count):
        return heads.at[i, :, pl.ds(pl.multiple_of(first, 128), count)]

    def d_copy(i, l):
        h, f = i // NF, i % NF
        there = d if h == 0 else mirror
        block = feats.at[f, yh, pl.ds(pl.multiple_of(yl * HD, 32), HD), :]
        return remote(d_src(i, l * RUN, RUN), block, d_send.at[i], d_recv.at[f], dev(h, there, l, z))

    def d_start(i):
        total = acc[i]
        heads[i] = (total[:, :HD] / total[:, HD : HD + 1]).astype(jnp.bfloat16).T
        for k in range(1, YL):
            d_copy(i, lax.rem(yl + k, YL)).start()
        if i < NF:

            @pl.when(yh == 0)
            def _():
                block = feats.at[i, yh, pl.ds(pl.multiple_of(yl * HD, 32), HD), :]
                pltpu.make_async_copy(d_src(i, yl * RUN, RUN), block, d_recv.at[i]).start()

            @pl.when(yh == 1)
            def _():
                d_copy(i, yl).start()
        else:
            d_copy(i, yl).start()

    def d_drain(i):
        if i < NF:

            @pl.when(yh == 0)
            def _():
                take(d_src(i, 0, FRAME_TOK - RUN), d_send.at[i])

            @pl.when(yh == 1)
            def _():
                take(d_src(i, 0, FRAME_TOK), d_send.at[i])
        else:
            take(d_src(i, 0, FRAME_TOK), d_send.at[i])

    def e_src(f, first, count):
        return spun.at[f, :, pl.ds(pl.multiple_of(first, TOK), count), :]

    def e_start(f):
        take(feats.at[f], d_recv.at[f])
        for clip in range(CLIPS):
            spun[f, clip] = feats[f, clip].T
        mine = rows.at[:, f, :, pl.ds(pl.multiple_of(z * GROUP, 128), GROUP)]
        for zz in z_peers:
            remote(e_src(f, zz * TOK, TOK), mine, e_send.at[f], e_recv.at[f], dev(yh, d, yl, zz)).start()
        pltpu.make_async_copy(e_src(f, z * TOK, TOK), mine, e_recv.at[f]).start()

    def e_finish(f):
        take(rows.at[:, f], e_recv.at[f])
        for clip in range(CLIPS):
            context = rows[clip, f].astype(jnp.float32)
            inverse_rms = lax.rsqrt(jnp.mean(context * context, axis=-1, keepdims=True) + 1e-06)
            out[clip, f] = (context * inverse_rms).astype(jnp.bfloat16)

    for t in range(5):
        a_start(t)
    a_wait(key0)
    b_start(key0)
    a_wait(value0)
    b_start(value0)
    c_start(key0)
    a_wait(query)
    b_start(query)
    c_start(value0)
    c_relay(key0)
    a_wait(key1)
    b_start(key1)
    c_relay(value0)
    a_wait(value1)
    b_start(value1)
    b_wait(query)
    prepare()
    c_start(key1)
    c_last(key0)
    c_ready(0, 4)
    visit(x, 0)
    c_start(value1)
    c_last(value0)
    c_ready(0, 5)
    visit(lax.rem(x + NX - 1, NX), 0)
    c_relay(key1)
    c_ready(0, 6)
    visit(lax.rem(x + 1, NX), 0)
    c_relay(value1)
    c_last(key1)
    c_ready(0, 7)
    visit(lax.rem(x + 2, NX), 0)
    for t in range(5):
        a_drain(t)
        b_drain(t)
    c_last(value1)
    for kind in (4, 5, 6, 7):
        c_ready(1, kind)
    for i in (0, 2, 1):
        sweep(i, 1, 0, YH * NX // 2)
        d_start(i)
    sweep(3, 1, 0, 2)
    e_start(0)
    sweep(3, 1, 2, YH * NX // 2)
    d_start(3)
    for t in (key0, value0, key1, value1):
        c_drain(t)
    e_start(1)
    for i in range(NF_Q):
        d_drain(i)
    e_finish(0)
    e_finish(1)
    for f in range(NF):
        take(e_src(f, 0, RUN - TOK), e_send.at[f])


def on_device(queries, keys, values, segment_ids):
    hbm = pl.BlockSpec(memory_space=pltpu.HBM)
    vmem = pl.BlockSpec(memory_space=pltpu.VMEM)
    gathered = pltpu.VMEM((YH, ND, NF, HD, FRAME_TOK), jnp.bfloat16)
    state = pltpu.VMEM((NF_Q, FRAME_TOK, 128), jnp.float32)
    dma = pltpu.SemaphoreType.DMA
    return pl.pallas_call(
        kernel,
        out_shape=jax.ShapeDtypeStruct((CLIPS, NF, TOK, NZ * GROUP), jnp.bfloat16),
        in_specs=[pl.BlockSpec(memory_space=pltpu.SMEM), hbm, hbm, hbm],
        out_specs=vmem,
        scratch_shapes=[
            gathered,
            gathered,
            pltpu.VMEM((YH, NF, HD, FRAME_TOK), jnp.bfloat16),
            pltpu.VMEM((5, CLIPS, RUN, GROUP), jnp.bfloat16),
            pltpu.VMEM((CLIPS, NF, RUN, GROUP), jnp.bfloat16),
            pltpu.VMEM((5, CLIPS * GROUP, RUN), jnp.bfloat16),
            pltpu.VMEM((NF, CLIPS * GROUP, RUN), jnp.bfloat16),
            pltpu.VMEM((NF_Q, FRAME_TOK, DEPTH), jnp.bfloat16),
            state,
            state,
            pltpu.VMEM((2, NCORE, FRAME_TOK, FRAME_TOK), jnp.float32),
            pltpu.VMEM((NF_Q, HD, FRAME_TOK), jnp.bfloat16),
            pltpu.VMEM((NF, CLIPS, GROUP, RUN), jnp.bfloat16),
            pltpu.VMEM((NF, CLIPS, RUN, GROUP), jnp.bfloat16),
            pltpu.VMEM((CLIPS, NF, TOK, NZ * GROUP), jnp.bfloat16),
            dma((5,)),
            dma((5,)),
            dma((5,)),
            dma((5,)),
            dma((5,)),
            dma((5, 8)),
            dma((NF_Q,)),
            dma((NF,)),
            dma((NF,)),
            dma((NF,)),
        ],
        compiler_params=pltpu.CompilerParams(collective_id=0, has_side_effects=True, vmem_limit_bytes=56 << 20),
        name="attend",
    )(segment_ids, keys, values, queries)


def solution(mesh):
    rows = P(None, "frames", "tiles", None)
    return jax.shard_map(
        on_device,
        mesh=mesh,
        in_specs=(rows, rows, rows, P()),
        out_specs=rows,
        check_vma=False,
    )
```

time: 104 us -> 101 us (0.971)
  Pallas kernels: 102 us -> 99 us
    pallas_call x1, Pallas kernels: 102 us -> 99 us  [on_device(): pl.pallas_call(kernel, out_shape=jax.ShapeDtypeStruct((CLIPS, NF, TOK, NZ...]
where the time goes in v3:
time: 101 us
  Pallas kernels  99 us (98%)
  local copies, waits for them, and re-layouts  1.77 us (2%)
    pallas_call x1, Pallas kernels, on_device(): pl.pallas_call(kernel, out_shape=jax.ShapeDtypeStruct((CLIPS, NF, TOK, NZ...  99 us

profile of v3, /device:TPU:56, one launch (start us, length us, event | category | flops | bytes accessed | tf_op | source)
XLA Modules:
  0.0 100.8 jit_solution(9445303205908135479)
XLA Ops:
  0.0 99.0 %attend.1 = bf16[2,2,16,3072]{3,2,1,0:T(8,128)(2,1)} custom-call(s32[2,32]{1,0:T(2,128)} %seg.1, bf16[2,2,16,3072]{3,2,1,0:T(8,128)(2,1)} %k_in.1, bf16[2,2,16,3072]{3,2,1,0:T(8,128)(2,1)} %v_in.1, bf16[2,2,16,3072]{3,2,1,0:T(8,128)(2,1)} %q_in.1), custom_call_target="tpu_custom_call" | custom-call | tf_op jit(solution)/shard_map/attend/pallas_call | solution.py:399
  99.0 1.8 %copy.6 = bf16[2,2,16,3072]{3,2,1,0:T(8,128)(2,1)} copy(bf16[2,2,16,3072]{3,2,1,0:T(8,128)(2,1)} %attend.1) | data formatting | bytes 786432
